TPU v7x, 32 devices: a whole 2x2x4 slice. The times are simulated.
32 devices in a mesh: lat: 4 (over x, core), tm: 8 (over z, y).
Axes of the slice: x: 2, y: 2, z: 4, core: 2. Of those that a mesh axis runs over, the one named last changes fastest.
Arguments:
- data: float32 [8, 128, 23040], P(None, 'tm', 'lat'), may hold values from -6 to 6
- space_init: float32 [32, 23040], P(None, 'lat'), may hold values from -0.0390625 to 0.0390625
- time_init: float32 [32, 128], P(None, 'tm'), may hold values from -6 to 6
- variable_factor: float32 [8, 32], replicated, may hold values from -2 to 2
- neighbours: int32 [4, 23040], P(None, 'lat'), may hold values from -1 to 23039, as said below
Outputs:
- time_factor: float32 [32, 128], P(None, 'tm')
- space_factor: float32 [32, 23040], P(None, 'lat')
Inputs may be any that keep to these rules, and one draw needn't show every extreme that they name: `neighbours`: points are numbered row by row: latitude row i holds points i * 360 to (i + 1) * 360 - 1. Rows 0 and 1 name the east and west neighbour in the same latitude row (cyclic in longitude); rows 2 and 3 name a point of the latitude row before and after, at most one column away (cyclic); -1 where the grid has no such row.
All inputs are finite; a program needn't handle non-finite values.
Results may differ from a plain program's by a relative error of at most 0.0001.
Values sent between devices are 32-bit elements; how exact they have to be, the bound alone decides.
A program may use at most 64 MiB of HBM per device.

v0:
```python
import jax
import jax.numpy as jnp
from jax import lax
from jax.sharding import PartitionSpec as P

NLON = 360
SWEEPS = 8


def padded_2(cells, sides, width):
    for axis, dim in sides:
        count = lax.axis_size(axis)
        ends = count - 1
        head = lax.slice_in_dim(cells, 0, width, axis=dim)
        tail = lax.slice_in_dim(cells, cells.shape[dim] - width, cells.shape[dim], axis=dim)
        cells = jnp.concatenate(
            [
                lax.ppermute(tail, axis, [(i, (i + 1) % count) for i in range(ends)]),
                cells,
                lax.ppermute(head, axis, [((i + 1) % count, i) for i in range(ends)]),
            ],
            axis=dim,
        )
    return cells


def inverse(matrix):
    lower = jnp.linalg.cholesky(matrix)
    identity = jnp.eye(matrix.shape[0], dtype=jnp.float32)
    return jax.scipy.linalg.cho_solve((lower, True), identity)


def link_masks(link, column, row_count):
    target = (link % NLON - column + NLON) % NLON
    ahead = (target == 1).reshape(row_count, NLON)
    behind = (target == NLON - 1).reshape(row_count, NLON)
    present = (link >= 0).reshape(row_count, NLON)
    return (ahead, behind, present)


def pick_row(block, masks):
    ahead, behind, present = masks
    moved = jnp.where(
        ahead[None],
        jnp.roll(block, -1, axis=2),
        jnp.where(behind[None], jnp.roll(block, 1, axis=2), block),
    )
    return jnp.where(present[None], moved, jnp.float32(0.0))


def run_sweeps(extend, start_factor, point_rhs, point_inv, neighbours):
    highest = lax.Precision.HIGHEST
    rank_count, point_count = start_factor.shape
    row_count = point_count // NLON
    column = jnp.arange(point_count, dtype=jnp.int32) % NLON
    north_masks = link_masks(neighbours[2], column, row_count)
    south_masks = link_masks(neighbours[3], column, row_count)
    current = start_factor
    for sweep_index in range(SWEEPS):
        extended = extend(current).reshape(rank_count, row_count + 2, NLON)
        center = extended[:, 1:-1]
        near_sum = jnp.roll(center, -1, axis=2) + jnp.roll(center, 1, axis=2)
        near_sum = (
            near_sum
            + pick_row(extended[:, :-2], north_masks)
            + pick_row(extended[:, 2:], south_masks)
        )
        near_sum = near_sum.reshape(rank_count, point_count)
        current = jnp.dot(
            point_inv,
            point_rhs + 0.5 * near_sum,
            precision=highest,
            preferred_element_type=jnp.float32,
        )
    return current


def per_device(data, space_init, time_init, variable_factor, neighbours):
    highest = lax.Precision.HIGHEST
    var_count, hour_count, point_count = data.shape
    rank_count = space_init.shape[0]
    identity = jnp.eye(rank_count, dtype=jnp.float32)
    unfolded = data.reshape(var_count * hour_count, point_count)
    var_gram = jnp.dot(
        variable_factor.T, variable_factor, precision=highest, preferred_element_type=jnp.float32
    )
    local_gram = lax.dot_general(
        space_init,
        space_init,
        (((1,), (1,)), ((), ())),
        precision=highest,
        preferred_element_type=jnp.float32,
    )
    space_gram = lax.psum(local_gram, "lat")
    padded = padded_2(time_init, (("tm", 1),), 2)
    stencil = padded[:, :-4] - 4.0 * padded[:, 1:-3] - 4.0 * padded[:, 3:-1] + padded[:, 4:]
    projected = lax.dot_general(
        space_init,
        unfolded,
        (((1,), (1,)), ((), ())),
        precision=highest,
        preferred_element_type=jnp.float32,
    )
    projected = projected.reshape(rank_count, var_count, hour_count)
    rhs_terms = jnp.sum(projected * variable_factor.T[:, :, None], axis=1)
    time_inv = inverse(space_gram * var_gram + 3.0 * identity)
    time_rhs = lax.psum(rhs_terms, "lat")
    time_factor = jnp.dot(
        time_inv, time_rhs - 0.5 * stencil, precision=highest, preferred_element_type=jnp.float32
    )
    weighted = (variable_factor.T[:, :, None] * time_factor[:, None, :]).reshape(
        rank_count, var_count * hour_count
    )
    point_terms = jnp.dot(weighted, unfolded, precision=highest, preferred_element_type=jnp.float32)
    hour_gram = lax.dot_general(
        time_factor,
        time_factor,
        (((1,), (1,)), ((), ())),
        precision=highest,
        preferred_element_type=jnp.float32,
    )
    time_gram = lax.psum(hour_gram, "tm")
    scale = jnp.sqrt(jnp.diagonal(time_gram) + 1e-06)
    point_op = time_gram / (scale[:, None] * scale[None, :]) * var_gram + 2.0 * identity
    point_inv = inverse(point_op)
    point_rhs = lax.psum(point_terms, "tm") / scale[:, None]

    def extend_band(current):
        return padded_2(current, (("lat", 1),), NLON)

    space_factor = run_sweeps(extend_band, space_init, point_rhs, point_inv, neighbours)
    return (time_factor, space_factor)


def solution(mesh):
    placed = (P(None, "tm", "lat"), P(None, "lat"), P(None, "tm"), P(), P(None, "lat"))
    return jax.shard_map(
        per_device,
        mesh=mesh,
        in_specs=placed,
        out_specs=(P(None, "tm"), P(None, "lat")),
        check_vma=False,
    )
```

profile of v0, /device:TPU:1, one launch (start us, length us, event | category | flops | bytes accessed | tf_op | source)
XLA Modules:
  0.0 271.1 jit_solution(8061384592421640205)
XLA Ops:
  8.1 1.4 collective-permute-start.1
  9.5 4.6 %collective-permute-start = (f32[32,2]{0,1:T(2,128)S(1)}, f32[32,2]{0,1:T(2,128)S(1)}, u32[]{:S(2)}, u32[]{:S(2)}) collective-permute-start(f32[32,2]{0,1:T(2,128)S(1)} %get-tuple-element.127), channel_id=1, source_target_pairs={{0,1},{1,2},{2,3},{3,4},{4,5},{5,6},{6,7},{8,9},{9,10},{10,11},{11... | collective-permute-start | bytes 776 | tf_op jit(solution)/shard_map/ppermute | solution.py:18
  15.1 2.9 %collective-permute-start.3 = (f32[32,360]{1,0:T(8,128)S(1)}, f32[32,360]{1,0:T(8,128)S(1)}, u32[]{:S(2)}, u32[]{:S(2)}) collective-permute-start(f32[32,360]{1,0:T(8,128)S(1)} %get-tuple-element.120), channel_id=1, source_target_pairs={{8,0},{16,8},{24,16},{9,1},{17,9},{25,17},{10,2},{18,10},{26,18},{... | collective-permute-start | bytes 138248 | tf_op jit(solution)/shard_map/ppermute | solution.py:20
  17.9 3.5 %collective-permute-start.2 = (f32[32,360]{1,0:T(8,128)S(1)}, f32[32,360]{1,0:T(8,128)S(1)}, u32[]{:S(2)}, u32[]{:S(2)}) collective-permute-start(f32[32,360]{1,0:T(8,128)S(1)} %get-tuple-element.121), channel_id=1, source_target_pairs={{0,8},{8,16},{16,24},{1,9},{9,17},{17,25},{2,10},{10,18},{18,26},{... | collective-permute-start | bytes 138248 | tf_op jit(solution)/shard_map/ppermute | solution.py:18
  22.1 2.2 fusion.142
  24.8 2.5 fusion
  27.3 10.3 %all-reduce = (f32[32,32]{0,1:T(8,128)S(1)}, f32[32,16]{0,1:T(8,128)S(1)}) all-reduce(f32[32,32]{0,1:T(8,128)S(1)} %fusion.142, f32[32,16]{0,1:T(8,128)S(1)} %fusion), channel_id=1, replica_groups=mesh['lat'=4,'tm'=8] {'lat'}, use_global_device_ids=true, to_apply=%region_0.0 | all-reduce | flops 1536 | bytes 12288 | tf_op jit(solution)/shard_map/psum | solution.py:94
  37.9 2.9 %cholesky.44 = f32[32,32]{1,0:T(8,128)S(1)} custom-call(f32[32,32]{1,0:T(8,128)S(1)} %fusion.99), custom_call_target="Cholesky" | custom-call | tf_op jit(solution)/shard_map/jit(cholesky)/cholesky | solution.py:28
  42.2 2.4 custom-call.10
  46.0 28.8 %psum.30 = f32[32,32]{0,1:T(8,128)S(1)} all-reduce(f32[32,32]{0,1:T(8,128)S(1)} %fusion.143), channel_id=1, replica_groups=mesh['lat'=4,'tm'=8] {'tm'}, use_global_device_ids=true, to_apply=%region_5.8 | all-reduce | flops 1024 | bytes 8192 | tf_op jit(solution)/shard_map/psum | solution.py:122
  75.7 2.9 %cholesky.55 = f32[32,32]{1,0:T(8,128)S(1)} custom-call(f32[32,32]{1,0:T(8,128)S(1)} %fusion.95), custom_call_target="Cholesky" | custom-call | tf_op jit(solution)/shard_map/jit(cholesky)/cholesky | solution.py:28
  80.0 2.4 custom-call.11
  82.8 2.5 convolution_bitcast_fusion
  88.4 1.9 fusion.53
  90.3 1.4 mul.128
  91.8 70.7 %all-reduce.3.cloned.1.call-done = f32[32,5760]{1,0:T(8,128)} async-done(((f32[32,5760]{1,0:T(8,128)}), f32[32,5760]{1,0:T(8,128)}) %all-reduce.3.cloned.1.call-update) | async-done | bytes 737296 | tf_op jit(solution)/shard_map/psum | solution.py:126
  162.4 1.9 fusion.72
  164.4 3.8 %collective-permute-start.5 = (f32[32,360]{1,0:T(8,128)S(1)}, f32[32,360]{1,0:T(8,128)S(1)}, u32[]{:S(2)}, u32[]{:S(2)}) collective-permute-start(f32[32,360]{1,0:T(8,128)S(1)} %get-tuple-element.118), channel_id=1, source_target_pairs={{8,0},{16,8},{24,16},{9,1},{17,9},{25,17},{10,2},{18,10},{26,18},{... | collective-permute-start | bytes 138248 | tf_op jit(solution)/shard_map/ppermute | solution.py:20
  168.3 3.0 %collective-permute-start.4 = (f32[32,360]{1,0:T(8,128)S(1)}, f32[32,360]{1,0:T(8,128)S(1)}, u32[]{:S(2)}, u32[]{:S(2)}) collective-permute-start(f32[32,360]{1,0:T(8,128)S(1)} %get-tuple-element.119), channel_id=1, source_target_pairs={{0,8},{8,16},{16,24},{1,9},{9,17},{17,25},{2,10},{10,18},{18,26},{... | collective-permute-start | bytes 138248 | tf_op jit(solution)/shard_map/ppermute | solution.py:18
  174.4 1.9 fusion.46
  176.3 1.5 mul.130
  178.7 1.9 collective-permute-start.7
  180.7 4.5 %collective-permute-start.6 = (f32[32,360]{1,0:T(8,128)S(1)}, f32[32,360]{1,0:T(8,128)S(1)}, u32[]{:S(2)}, u32[]{:S(2)}) collective-permute-start(f32[32,360]{1,0:T(8,128)S(1)} %get-tuple-element.117), channel_id=1, source_target_pairs={{0,8},{8,16},{16,24},{1,9},{9,17},{17,25},{2,10},{10,18},{18,26},{... | collective-permute-start | bytes 138248 | tf_op jit(solution)/shard_map/ppermute | solution.py:18
  188.1 1.9 fusion.39
  190.0 1.5 mul.132
  192.4 1.9 collective-permute-start.9
  194.3 4.2 %collective-permute-start.8 = (f32[32,360]{1,0:T(8,128)S(1)}, f32[32,360]{1,0:T(8,128)S(1)}, u32[]{:S(2)}, u32[]{:S(2)}) collective-permute-start(f32[32,360]{1,0:T(8,128)S(1)} %get-tuple-element.115), channel_id=1, source_target_pairs={{0,8},{8,16},{16,24},{1,9},{9,17},{17,25},{2,10},{10,18},{18,26},{... | collective-permute-start | bytes 138248 | tf_op jit(solution)/shard_map/ppermute | solution.py:18
  198.6 1.1 collective-permute-done.8
  201.8 1.9 fusion.32
  203.7 1.5 mul.134
  206.1 1.9 collective-permute-start.11
  208.0 4.2 %collective-permute-start.10 = (f32[32,360]{1,0:T(8,128)S(1)}, f32[32,360]{1,0:T(8,128)S(1)}, u32[]{:S(2)}, u32[]{:S(2)}) collective-permute-start(f32[32,360]{1,0:T(8,128)S(1)} %get-tuple-element.113), channel_id=1, source_target_pairs={{0,8},{8,16},{16,24},{1,9},{9,17},{17,25},{2,10},{10,18},{18,26},{... | collective-permute-start | bytes 138248 | tf_op jit(solution)/shard_map/ppermute | solution.py:18
  215.5 1.9 fusion.25
  217.3 1.5 mul.136
  219.8 1.9 collective-permute-start.13
  221.7 4.5 %collective-permute-start.12 = (f32[32,360]{1,0:T(8,128)S(1)}, f32[32,360]{1,0:T(8,128)S(1)}, u32[]{:S(2)}, u32[]{:S(2)}) collective-permute-start(f32[32,360]{1,0:T(8,128)S(1)} %get-tuple-element.111), channel_id=1, source_target_pairs={{0,8},{8,16},{16,24},{1,9},{9,17},{17,25},{2,10},{10,18},{18,26},{... | collective-permute-start | bytes 138248 | tf_op jit(solution)/shard_map/ppermute | solution.py:18
  229.1 1.9 fusion.18
  231.0 1.5 mul.138
  233.4 1.9 collective-permute-start.15
  235.4 4.2 %collective-permute-start.14 = (f32[32,360]{1,0:T(8,128)S(1)}, f32[32,360]{1,0:T(8,128)S(1)}, u32[]{:S(2)}, u32[]{:S(2)}) collective-permute-start(f32[32,360]{1,0:T(8,128)S(1)} %get-tuple-element.109), channel_id=1, source_target_pairs={{0,8},{8,16},{16,24},{1,9},{9,17},{17,25},{2,10},{10,18},{18,26},{... | collective-permute-start | bytes 138248 | tf_op jit(solution)/shard_map/ppermute | solution.py:18
  239.6 1.1 collective-permute-done.14
  242.8 1.9 fusion.11
  244.7 1.5 mul.140
  247.1 1.9 collective-permute-start.17
  249.0 4.2 %collective-permute-start.16 = (f32[32,360]{1,0:T(8,128)S(1)}, f32[32,360]{1,0:T(8,128)S(1)}, u32[]{:S(2)}, u32[]{:S(2)}) collective-permute-start(f32[32,360]{1,0:T(8,128)S(1)} %get-tuple-element.107), channel_id=1, source_target_pairs={{0,8},{8,16},{16,24},{1,9},{9,17},{17,25},{2,10},{10,18},{18,26},{... | collective-permute-start | bytes 138248 | tf_op jit(solution)/shard_map/ppermute | solution.py:18
  256.5 1.9 fusion.4
  258.4 2.5 mul.142
  260.8 3.0 %fusion.58 = f32[32,5760]{1,0:T(8,128)} fusion(f32[32,32]{1,0:T(8,128)S(1)} %fusion.92, f32[32,5760]{1,0:T(8,128)} %mul.142, f32[32,5760]{1,0:T(8,128)} %all-reduce.3.cloned.1.call-done, f32[32]{0:T(128)S(1)} %add_sqrt_fusion), kind=kOutput, calls=%fused_computation.85 | convolution fusion | flops 71147520 | bytes 2216064 | tf_op jit(solution)/shard_map/dot_general | solution.py:69
  (123 shorter events, 36.4 us)
Async XLA Ops:
  7.2 17.6 %copy-start = (f32[8,16,5760]{2,1,0:T(8,128)S(1)}, f32[8,16,5760]{2,1,0:T(8,128)}, u32[]{:S(2)}) copy-start(f32[8,16,5760]{2,1,0:T(8,128)} %param.8) | copy-start | bytes 8847364
  7.2 17.1 %copy-start.4 = (s32[4,5760]{1,0:T(4,128)S(1)}, s32[4,5760]{1,0:T(4,128)}, u32[]{:S(2)}) copy-start(s32[4,5760]{1,0:T(4,128)} %param.12) | copy-start | bytes 276484
  7.2 17.6 %copy-start.7 = (f32[8,32]{1,0:T(8,128)S(1)}, f32[8,32]{1,0:T(8,128)}, u32[]{:S(2)}) copy-start(f32[8,32]{1,0:T(8,128)} %param.11) | copy-start | bytes 3076
  7.2 155.2 %all-reduce.3.cloned.1.call-start = ((), (), s32[]{:S(2)}) async-start(), calls=%async_computation | async-start | bytes 1474560 | tf_op jit(solution)/shard_map/psum | solution.py:126
  7.2 17.6 %copy-start.2 = (f32[32,5760]{1,0:T(8,128)S(1)}, f32[32,5760]{1,0:T(8,128)}, u32[]{:S(2)}) copy-start(f32[32,5760]{1,0:T(8,128)} %param.9) | copy-start | bytes 2211844
  8.1 37.4 %collective-permute-start.1 = (f32[32,2]{0,1:T(2,128)S(1)}, f32[32,2]{0,1:T(2,128)S(1)}, u32[]{:S(2)}, u32[]{:S(2)}) collective-permute-start(f32[32,2]{0,1:T(2,128)S(1)} %get-tuple-element.126), channel_id=1, source_target_pairs={{1,0},{2,1},{3,2},{4,3},{5,4},{6,5},{7,6},{9,8},{10,9},{11,10},{12... | collective-permute-start | bytes 776 | tf_op jit(solution)/shard_map/ppermute | solution.py:20
  9.5 36.0 %collective-permute-start = (f32[32,2]{0,1:T(2,128)S(1)}, f32[32,2]{0,1:T(2,128)S(1)}, u32[]{:S(2)}, u32[]{:S(2)}) collective-permute-start(f32[32,2]{0,1:T(2,128)S(1)} %get-tuple-element.127), channel_id=1, source_target_pairs={{0,1},{1,2},{2,3},{3,4},{4,5},{5,6},{6,7},{8,9},{9,10},{10,11},{11... | collective-permute-start | bytes 776 | tf_op jit(solution)/shard_map/ppermute | solution.py:18
  15.1 70.2 %collective-permute-start.3 = (f32[32,360]{1,0:T(8,128)S(1)}, f32[32,360]{1,0:T(8,128)S(1)}, u32[]{:S(2)}, u32[]{:S(2)}) collective-permute-start(f32[32,360]{1,0:T(8,128)S(1)} %get-tuple-element.120), channel_id=1, source_target_pairs={{8,0},{16,8},{24,16},{9,1},{17,9},{25,17},{10,2},{18,10},{26,18},{... | collective-permute-start | bytes 138248 | tf_op jit(solution)/shard_map/ppermute | solution.py:20
  17.9 67.4 %collective-permute-start.2 = (f32[32,360]{1,0:T(8,128)S(1)}, f32[32,360]{1,0:T(8,128)S(1)}, u32[]{:S(2)}, u32[]{:S(2)}) collective-permute-start(f32[32,360]{1,0:T(8,128)S(1)} %get-tuple-element.121), channel_id=1, source_target_pairs={{0,8},{8,16},{16,24},{1,9},{9,17},{17,25},{2,10},{10,18},{18,26},{... | collective-permute-start | bytes 138248 | tf_op jit(solution)/shard_map/ppermute | solution.py:18
  24.8 20.8 %copy-start.5 = (f32[32,16]{0,1:T(8,128)S(1)}, f32[32,16]{0,1:T(8,128)}, u32[]{:S(2)}) copy-start(f32[32,16]{0,1:T(8,128)} %param.10) | copy-start | bytes 6148
  45.7 39.6 %copy-start.6 = (f32[32,16]{0,1:T(8,128)}, f32[32,16]{0,1:T(8,128)S(1)}, u32[]{:S(2)}) copy-start(f32[32,16]{0,1:T(8,128)S(1)} %fusion.106) | copy-start | bytes 6148
  85.3 1.1 copy-start.3
  164.4 6.8 %collective-permute-start.5 = (f32[32,360]{1,0:T(8,128)S(1)}, f32[32,360]{1,0:T(8,128)S(1)}, u32[]{:S(2)}, u32[]{:S(2)}) collective-permute-start(f32[32,360]{1,0:T(8,128)S(1)} %get-tuple-element.118), channel_id=1, source_target_pairs={{8,0},{16,8},{24,16},{9,1},{17,9},{25,17},{10,2},{18,10},{26,18},{... | collective-permute-start | bytes 138248 | tf_op jit(solution)/shard_map/ppermute | solution.py:20
  168.3 4.1 %collective-permute-start.4 = (f32[32,360]{1,0:T(8,128)S(1)}, f32[32,360]{1,0:T(8,128)S(1)}, u32[]{:S(2)}, u32[]{:S(2)}) collective-permute-start(f32[32,360]{1,0:T(8,128)S(1)} %get-tuple-element.119), channel_id=1, source_target_pairs={{0,8},{8,16},{16,24},{1,9},{9,17},{17,25},{2,10},{10,18},{18,26},{... | collective-permute-start | bytes 138248 | tf_op jit(solution)/shard_map/ppermute | solution.py:18
  176.3 1.5 copy-start.8
  178.7 6.4 %collective-permute-start.7 = (f32[32,360]{1,0:T(8,128)S(1)}, f32[32,360]{1,0:T(8,128)S(1)}, u32[]{:S(2)}, u32[]{:S(2)}) collective-permute-start(f32[32,360]{1,0:T(8,128)S(1)} %get-tuple-element.116), channel_id=1, source_target_pairs={{8,0},{16,8},{24,16},{9,1},{17,9},{25,17},{10,2},{18,10},{26,18},{... | collective-permute-start | bytes 138248 | tf_op jit(solution)/shard_map/ppermute | solution.py:20
  180.7 5.4 %collective-permute-start.6 = (f32[32,360]{1,0:T(8,128)S(1)}, f32[32,360]{1,0:T(8,128)S(1)}, u32[]{:S(2)}, u32[]{:S(2)}) collective-permute-start(f32[32,360]{1,0:T(8,128)S(1)} %get-tuple-element.117), channel_id=1, source_target_pairs={{0,8},{8,16},{16,24},{1,9},{9,17},{17,25},{2,10},{10,18},{18,26},{... | collective-permute-start | bytes 138248 | tf_op jit(solution)/shard_map/ppermute | solution.py:18
  190.0 1.5 copy-start.9
  192.4 6.2 %collective-permute-start.9 = (f32[32,360]{1,0:T(8,128)S(1)}, f32[32,360]{1,0:T(8,128)S(1)}, u32[]{:S(2)}, u32[]{:S(2)}) collective-permute-start(f32[32,360]{1,0:T(8,128)S(1)} %get-tuple-element.114), channel_id=1, source_target_pairs={{8,0},{16,8},{24,16},{9,1},{17,9},{25,17},{10,2},{18,10},{26,18},{... | collective-permute-start | bytes 138248 | tf_op jit(solution)/shard_map/ppermute | solution.py:20
  194.3 5.4 %collective-permute-start.8 = (f32[32,360]{1,0:T(8,128)S(1)}, f32[32,360]{1,0:T(8,128)S(1)}, u32[]{:S(2)}, u32[]{:S(2)}) collective-permute-start(f32[32,360]{1,0:T(8,128)S(1)} %get-tuple-element.115), channel_id=1, source_target_pairs={{0,8},{8,16},{16,24},{1,9},{9,17},{17,25},{2,10},{10,18},{18,26},{... | collective-permute-start | bytes 138248 | tf_op jit(solution)/shard_map/ppermute | solution.py:18
  203.7 1.5 copy-start.10
  206.1 6.2 %collective-permute-start.11 = (f32[32,360]{1,0:T(8,128)S(1)}, f32[32,360]{1,0:T(8,128)S(1)}, u32[]{:S(2)}, u32[]{:S(2)}) collective-permute-start(f32[32,360]{1,0:T(8,128)S(1)} %get-tuple-element.112), channel_id=1, source_target_pairs={{8,0},{16,8},{24,16},{9,1},{17,9},{25,17},{10,2},{18,10},{26,18},{... | collective-permute-start | bytes 138248 | tf_op jit(solution)/shard_map/ppermute | solution.py:20
  208.0 5.4 %collective-permute-start.10 = (f32[32,360]{1,0:T(8,128)S(1)}, f32[32,360]{1,0:T(8,128)S(1)}, u32[]{:S(2)}, u32[]{:S(2)}) collective-permute-start(f32[32,360]{1,0:T(8,128)S(1)} %get-tuple-element.113), channel_id=1, source_target_pairs={{0,8},{8,16},{16,24},{1,9},{9,17},{17,25},{2,10},{10,18},{18,26},{... | collective-permute-start | bytes 138248 | tf_op jit(solution)/shard_map/ppermute | solution.py:18
  217.3 1.5 copy-start.11
  219.8 6.4 %collective-permute-start.13 = (f32[32,360]{1,0:T(8,128)S(1)}, f32[32,360]{1,0:T(8,128)S(1)}, u32[]{:S(2)}, u32[]{:S(2)}) collective-permute-start(f32[32,360]{1,0:T(8,128)S(1)} %get-tuple-element.110), channel_id=1, source_target_pairs={{8,0},{16,8},{24,16},{9,1},{17,9},{25,17},{10,2},{18,10},{26,18},{... | collective-permute-start | bytes 138248 | tf_op jit(solution)/shard_map/ppermute | solution.py:20
  221.7 5.4 %collective-permute-start.12 = (f32[32,360]{1,0:T(8,128)S(1)}, f32[32,360]{1,0:T(8,128)S(1)}, u32[]{:S(2)}, u32[]{:S(2)}) collective-permute-start(f32[32,360]{1,0:T(8,128)S(1)} %get-tuple-element.111), channel_id=1, source_target_pairs={{0,8},{8,16},{16,24},{1,9},{9,17},{17,25},{2,10},{10,18},{18,26},{... | collective-permute-start | bytes 138248 | tf_op jit(solution)/shard_map/ppermute | solution.py:18
  231.0 1.5 copy-start.12
  233.4 6.2 %collective-permute-start.15 = (f32[32,360]{1,0:T(8,128)S(1)}, f32[32,360]{1,0:T(8,128)S(1)}, u32[]{:S(2)}, u32[]{:S(2)}) collective-permute-start(f32[32,360]{1,0:T(8,128)S(1)} %get-tuple-element.108), channel_id=1, source_target_pairs={{8,0},{16,8},{24,16},{9,1},{17,9},{25,17},{10,2},{18,10},{26,18},{... | collective-permute-start | bytes 138248 | tf_op jit(solution)/shard_map/ppermute | solution.py:20
  235.4 5.4 %collective-permute-start.14 = (f32[32,360]{1,0:T(8,128)S(1)}, f32[32,360]{1,0:T(8,128)S(1)}, u32[]{:S(2)}, u32[]{:S(2)}) collective-permute-start(f32[32,360]{1,0:T(8,128)S(1)} %get-tuple-element.109), channel_id=1, source_target_pairs={{0,8},{8,16},{16,24},{1,9},{9,17},{17,25},{2,10},{10,18},{18,26},{... | collective-permute-start | bytes 138248 | tf_op jit(solution)/shard_map/ppermute | solution.py:18
  244.7 1.5 copy-start.13
  247.1 6.2 %collective-permute-start.17 = (f32[32,360]{1,0:T(8,128)S(1)}, f32[32,360]{1,0:T(8,128)S(1)}, u32[]{:S(2)}, u32[]{:S(2)}) collective-permute-start(f32[32,360]{1,0:T(8,128)S(1)} %get-tuple-element.106), channel_id=1, source_target_pairs={{8,0},{16,8},{24,16},{9,1},{17,9},{25,17},{10,2},{18,10},{26,18},{... | collective-permute-start | bytes 138248 | tf_op jit(solution)/shard_map/ppermute | solution.py:20
  249.0 5.4 %collective-permute-start.16 = (f32[32,360]{1,0:T(8,128)S(1)}, f32[32,360]{1,0:T(8,128)S(1)}, u32[]{:S(2)}, u32[]{:S(2)}) collective-permute-start(f32[32,360]{1,0:T(8,128)S(1)} %get-tuple-element.107), channel_id=1, source_target_pairs={{0,8},{8,16},{16,24},{1,9},{9,17},{17,25},{2,10},{10,18},{18,26},{... | collective-permute-start | bytes 138248 | tf_op jit(solution)/shard_map/ppermute | solution.py:18
  258.4 5.5 %copy-start.1 = (f32[8,16,5760]{2,1,0:T(8,128)S(1)}, f32[8,16,5760]{2,1,0:T(8,128)}, u32[]{:S(2)}) copy-start(f32[8,16,5760]{2,1,0:T(8,128)} %param.8) | copy-start | bytes 8847364
Sparse Core Ops, SparseCore 0:
  85.4 76.9 all-reduce.2
where the time goes:
time: 277 us; the launch traced here: 271 us
  waiting for transfers between devices  78.3 us (28%)
  starting transfers between devices  56.6 us (20%)
  blocking collectives  39.2 us (14%)
  local copies, waits for them, and re-layouts  34.6 us (12%)
  other arithmetic  29 us (10%)
  matrix products  18.2 us (7%)
  between operations  15.3 us (6%)
    psum x1, waiting for transfers between devices, per_device(): point_rhs = lax.psum(point_terms, 'tm') / scale[:, None]  70.7 us
    ppermute x9, starting transfers between devices, padded_2(): lax.ppermute(tail, axis, [(i, (i + 1) % count) for i in range(ends)])  37 us
    psum x1, blocking collectives, per_device(): time_gram = lax.psum(hour_gram, 'tm')  28.8 us
    ppermute x9, starting transfers between devices, padded_2(): lax.ppermute(head, axis, [((i + 1) % count, i) for i in range(ends)])  19.6 us
    mul x8, other arithmetic, run_sweeps(): 0.5 * near_sum  15 us
    mul x8, local copies, waits for them, and re-layouts, run_sweeps(): 0.5 * near_sum  13 us
    psum x1, blocking collectives, per_device(): space_gram = lax.psum(local_gram, 'lat')  10.3 us
    dot_general x8, matrix products, run_sweeps(): jnp.dot(point_inv, point_rhs + 0.5 * near_sum, precision=highest, preferr...  9.77 us
  transfers between devices with their start and end apart: 19, of which 8 were waited for; matrix products, arithmetic and copies ran while one was open for 11% of the time, Pallas kernels for 0%

commit v1 on v0

v1 whole, which is shorter than its diff:
```python
import functools

import jax
import jax.numpy as jnp
import numpy as np
from jax import lax
from jax.experimental import pallas as pl
from jax.experimental.pallas import tpu as pltpu
from jax.sharding import PartitionSpec as P

NLON = 360
SWEEPS = 8
WIDE = 384
SIDE = (WIDE - NLON) // 2
WINDOW = 512
F32 = jnp.float32
BF16 = jnp.bfloat16
HIGHEST = lax.Precision.HIGHEST
MESH = pl.DeviceIdType.MESH
NN = (((1,), (0,)), ((), ()))
NT = (((1,), (1,)), ((), ()))
TN = (((0,), (0,)), ((), ()))


def exact_dot(a, b, dims=NN):
    return lax.dot_general(a, b, dims, precision=HIGHEST, preferred_element_type=F32)


def halves(x):
    high = x.astype(BF16)
    return high, (x - high.astype(F32)).astype(BF16)


def left_stack(x):
    high, low = halves(x)
    return jnp.concatenate([high, high, low], axis=1)


def split_dot(stack, b):
    high, low = halves(b)
    return jnp.dot(stack, jnp.concatenate([high, low, high], axis=0), preferred_element_type=F32)


def inverse(matrix, row_id, col_id):
    for k in range(matrix.shape[0]):
        pivot = 1.0 / matrix[k : k + 1, k : k + 1]
        row = jnp.where(col_id[:1] == k, 1.0, matrix[k : k + 1, :]) * pivot
        rest = jnp.where(col_id == k, 0.0, matrix) - matrix[:, k : k + 1] * row
        matrix = jnp.where(row_id == k, row, rest)
    return matrix


def window_of(row, total):
    start = min(row * NLON // 128 * 128, total - WINDOW)
    return start, row * NLON - start


def spread_row(load, row, total, lane):
    start, shift = window_of(row, total)
    cells = load(start)
    if shift:
        cells = pltpu.roll(cells, WINDOW - shift, 1)
    cells = cells[:, :WIDE]
    after = pltpu.roll(cells, NLON, 1)
    before = pltpu.roll(cells, WIDE - NLON, 1)
    return jnp.where(lane < NLON, cells, jnp.where(lane < NLON + SIDE, after, before))


def kernel(
    lats, tms, data_ref, space_ref, time_ref, var_ref, links_ref, expand_ref, tile_ref, taps_ref,
    time_out, space_out,
    small, small_in, edge, edge_in, gram, gram_in, flat, terms, terms_in, rhs, codes,
    centre, east, west,
    small_s, small_r, edge_s, edge_r, halo_s, halo_r, gram_s, gram_r, rs_s, rs_r, ag_s, ag_r, fw_s, fw_r,
):
    lat, tm = lax.axis_index("lat"), lax.axis_index("tm")
    rank, points = space_ref.shape
    hours = time_ref.shape[1]
    rows = points // NLON
    deep = SWEEPS
    extent = rows + 2 * deep
    share = rows // tms
    north, south = lat > 0, lat < lats - 1

    def to_lat(offset):
        return {"lat": lax.rem(lat + offset, lats)}

    def to_tm(offset):
        return {"tm": lax.rem(tm + offset, tms)}

    def send(src, dst, send_sem, recv_sem, device):
        return pltpu.make_async_remote_copy(
            src_ref=src, dst_ref=dst, send_sem=send_sem, recv_sem=recv_sem,
            device_id=device, device_id_type=MESH,
        )

    barrier = pltpu.get_barrier_semaphore()
    for d in range(1, lats):
        pl.semaphore_signal(barrier, inc=1, device_id=to_lat(d), device_id_type=MESH)
    for d in range(1, tms):
        pl.semaphore_signal(barrier, inc=1, device_id=to_tm(d), device_id_type=MESH)

    edge[...] = jnp.zeros_like(edge)
    edge[:, :hours] = time_ref[...]
    pl.semaphore_wait(barrier, lats + tms - 2)
    up = send(edge, edge_in.at[0], edge_s.at[0], edge_r.at[0], to_tm(1))
    down = send(edge, edge_in.at[1], edge_s.at[1], edge_r.at[1], to_tm(tms - 1))
    up.start()
    down.start()

    chunk = points // 5

    def gather(i, sums):
        cells = pl.ds(pl.multiple_of(i * chunk, 128), chunk)
        mine = space_ref[:, cells]
        return (
            sums[0] + exact_dot(mine, data_ref[:, cells], NT),
            sums[1] + exact_dot(mine, mine, NT),
        )

    projected, local_gram = lax.fori_loop(
        0, 5, gather,
        (jnp.zeros((rank, data_ref.shape[0]), F32), jnp.zeros((rank, rank), F32)),
    )
    weights = exact_dot(var_ref[...], expand_ref[...], TN)
    small[...] = jnp.zeros_like(small)
    small[0, :, :rank] = local_gram
    small[1, :, :hours] = exact_dot(projected * weights, tile_ref[...], NT)
    small_sends = []
    for d in range(1, lats):
        copy = send(small, small_in.at[d], small_s.at[d], small_r.at[d], to_lat(d))
        copy.start()
        small_sends.append(copy)

    lane = lax.broadcasted_iota(jnp.int32, (rank, WIDE), 1)
    place = lax.broadcasted_iota(jnp.int32, (1, points), 1) + lat * points
    for side, step in ((0, -NLON), (1, NLON)):
        link = links_ref[2 + side : 3 + side, :]
        shift = link - (place + step)
        ahead = (shift == 1) | (shift == 1 - NLON)
        behind = (shift == -1) | (shift == NLON - 1)
        code = jnp.where(link < 0, 3.0, jnp.where(ahead, 1.0, jnp.where(behind, 2.0, 0.0)))
        flat[0:8, :] = jnp.broadcast_to(code, (8, points))
        for row in range(rows):
            codes[deep + row, side] = spread_row(
                lambda s: flat[0:8, s : s + WINDOW], row, points, lane[:8]
            )
    for row in range(rows):
        centre[0, deep + row] = spread_row(
            lambda s: space_ref[:, s : s + WINDOW], row, points, lane
        )
    top, bottom = pl.ds(deep, deep), pl.ds(rows, deep)
    before, behind_rows = pl.ds(0, deep), pl.ds(rows + deep, deep)
    halo = []
    for side, (exists, mine, theirs, offset) in enumerate(
        ((north, top, behind_rows, lats - 1), (south, bottom, before, 1))
    ):
        a = send(centre.at[0, mine], centre.at[0, theirs], halo_s.at[side, 0], halo_r.at[side, 0], to_lat(offset))
        b = send(codes.at[mine], codes.at[theirs], halo_s.at[side, 1], halo_r.at[side, 1], to_lat(offset))
        halo.append((exists, a, b))

        @pl.when(exists)
        def _(a=a, b=b):
            a.start()
            b.start()

    row_id = lax.broadcasted_iota(jnp.int32, (rank, rank), 0)
    col_id = lax.broadcasted_iota(jnp.int32, (rank, rank), 1)
    eye = jnp.where(row_id == col_id, F32(1.0), F32(0.0))
    var_gram = exact_dot(var_ref[...], var_ref[...], TN)
    up.wait()
    down.wait()
    past = jnp.where(tm > 0, edge_in[0, :, :hours], 0.0)
    coming = jnp.where(tm < tms - 1, edge_in[1, :, :hours], 0.0)
    stencil = (
        exact_dot(past, taps_ref[0]) + exact_dot(time_ref[...], taps_ref[1]) + exact_dot(coming, taps_ref[2])
    )
    total = small[...]
    for d, copy in enumerate(small_sends, 1):
        copy.wait()
        total = total + small_in[d]
    space_gram, time_rhs = total[0, :, :rank], total[1, :, :hours]
    time_inv = inverse(space_gram * var_gram + 3.0 * eye, row_id, col_id)
    time_factor = exact_dot(time_inv, time_rhs - 0.5 * stencil)
    time_out[...] = time_factor
    gram[...] = jnp.zeros_like(gram)
    gram[:, :rank] = exact_dot(time_factor, time_factor, NT)
    gram_sends = []
    for d in range(1, tms):
        copy = send(gram, gram_in.at[d], gram_s.at[d], gram_r.at[d], to_tm(d))
        copy.start()
        gram_sends.append(copy)

    stack = left_stack(weights * exact_dot(time_factor, tile_ref[...]))

    @pl.loop(0, 5)
    def _(i):
        cells = pl.ds(pl.multiple_of(i * chunk, 128), chunk)
        flat[:, cells] = split_dot(stack, data_ref[:, cells])

    for row in range(rows):
        terms[row] = spread_row(lambda s: flat[:, s : s + WINDOW], row, points, lane)
    rs_sends = []
    for d in range(1, tms):
        target = lax.rem(tm + d, tms)
        copy = send(terms.at[pl.ds(target * share, share)], terms_in.at[d], rs_s.at[d], rs_r.at[d], to_tm(d))
        copy.start()
        rs_sends.append(copy)

    time_gram = gram[:, :rank]
    for d, copy in enumerate(gram_sends, 1):
        copy.wait()
        time_gram = time_gram + gram_in[d, :, :rank]
    diagonal = time_gram * eye
    scale = jnp.sqrt(jnp.sum(diagonal, axis=1, keepdims=True) + 1e-06)
    scale_row = jnp.sqrt(jnp.sum(diagonal, axis=0, keepdims=True) + 1e-06)
    point_inv = inverse(time_gram / (scale * scale_row) * var_gram + 2.0 * eye, row_id, col_id)
    sweep_stack = left_stack(point_inv)

    mine = pl.ds(tm * share, share)
    owned = terms[mine]
    for d, copy in enumerate(rs_sends, 1):
        copy.wait_recv()
        owned = owned + terms_in[d]
    held = pl.ds(deep + tm * share, share)
    rhs[held] = owned / scale[None]
    ag_sends = []
    for d in range(1, tms):
        copy = send(rhs.at[held], rhs.at[held], ag_s.at[d], ag_r.at[d], to_tm(d))
        copy.start()
        ag_sends.append(copy)

    def shift_row(buf, row):
        cells = centre[buf, row]
        east[buf, row] = pltpu.roll(cells, WIDE - 1, 1)
        west[buf, row] = pltpu.roll(cells, 1, 1)

    for side, arrives in ((0, south), (1, north)):
        _, a, b = halo[side]

        @pl.when(arrives)
        def _(a=a, b=b):
            a.wait_recv()
            b.wait_recv()

    for exists, a, b in halo:

        @pl.when(exists)
        def _(a=a, b=b):
            a.wait_send()
            b.wait_send()

    @pl.loop(0, extent)
    def _(row):
        shift_row(0, row)

    def forward(source, start):
        block = source * share
        for side, exists, wanted, offset, move in (
            (0, north, block < deep, lats - 1, rows),
            (1, south, block + share > rows - deep, 1, -rows),
        ):
            place = deep + block + jnp.where(wanted, move, 0)
            copy = send(
                rhs.at[pl.ds(deep + block, share)], rhs.at[pl.ds(place, share)],
                fw_s.at[side, source], fw_r.at[side, source], to_lat(offset),
            )

            @pl.when(jnp.logical_and(exists, wanted))
            def _():
                if start:
                    copy.start()
                else:
                    copy.wait_send()

    forward(tm, True)
    for d, copy in enumerate(ag_sends, 1):
        copy.wait_recv()
        forward(lax.rem(tm + tms - d, tms), True)

    for side, arrives in ((0, south), (1, north)):
        for source in range(tms):
            block = source * share
            if (block < deep) if side == 0 else (block + share > rows - deep):
                move = rows if side == 0 else -rows
                copy = send(
                    rhs.at[pl.ds(deep + block, share)], rhs.at[pl.ds(deep + block + move, share)],
                    fw_s.at[side, source], fw_r.at[side, source], to_lat(1),
                )

                @pl.when(arrives)
                def _(copy=copy):
                    copy.wait_recv()

    def pick(buf, row, code):
        a = centre[buf, row].reshape(rank // 8, 8, WIDE)
        e = east[buf, row].reshape(rank // 8, 8, WIDE)
        w = west[buf, row].reshape(rank // 8, 8, WIDE)
        code = code[None]
        moved = jnp.where(code == 1.0, e, jnp.where(code == 2.0, w, a))
        return jnp.where(code == 3.0, 0.0, moved)

    for sweep in range(SWEEPS):
        now, later = sweep % 2, (sweep + 1) % 2
        least = sweep + 1

        def one(row, now=now, later=later, sweep=sweep):
            sides = (east[now, row] + west[now, row]).reshape(rank // 8, 8, WIDE)
            near = sides + pick(now, row - 1, codes[row, 0]) + pick(now, row + 1, codes[row, 1])
            cells = split_dot(sweep_stack, rhs[row] + 0.5 * near.reshape(rank, WIDE))
            centre[later, row] = cells
            if sweep < SWEEPS - 1:
                east[later, row] = pltpu.roll(cells, WIDE - 1, 1)
                west[later, row] = pltpu.roll(cells, 1, 1)

        @pl.loop(0, (extent - 2 * least) // 2)
        def _(i, one=one, least=least):
            one(least + 2 * i)
            one(least + 2 * i + 1)

    last = SWEEPS % 2
    wide_lane = lax.broadcasted_iota(jnp.int32, (rank, WINDOW), 1)
    for row in range(rows):
        start, shift = window_of(row, points)
        cells = jnp.concatenate([centre[last, deep + row], jnp.zeros((rank, WINDOW - WIDE), F32)], axis=1)
        if shift:
            cells = pltpu.roll(cells, shift, 1)
        inside = (wide_lane >= shift) & (wide_lane < shift + NLON)
        old = space_out[:, start : start + WINDOW]
        space_out[:, start : start + WINDOW] = jnp.where(inside, cells, old)

    for copy in rs_sends + ag_sends:
        copy.wait_send()
    for source in range(tms):
        forward(jnp.int32(source), False)


def per_device(lats, tms, data, space_init, time_init, variable_factor, neighbours):
    var_count, hours, points = data.shape
    rank = space_init.shape[0]
    rows = points // NLON
    extent = rows + 2 * SWEEPS
    share = rows // tms
    columns = np.arange(var_count * hours)
    expand = (columns[None] // hours == np.arange(var_count)[:, None]).astype(np.float32)
    tile = (columns[None] % hours == np.arange(hours)[:, None]).astype(np.float32)
    wide = np.zeros((3 * hours, hours), np.float32)
    for h in range(hours):
        for step, tap in ((-2, 1.0), (-1, -4.0), (1, -4.0), (2, 1.0)):
            wide[hours + h + step, h] = tap
    taps = wide.reshape(3, hours, hours)
    vmem = pl.BlockSpec(memory_space=pltpu.VMEM)
    dma = pltpu.SemaphoreType.DMA
    return pl.pallas_call(
        functools.partial(kernel, lats, tms),
        out_shape=(
            jax.ShapeDtypeStruct((rank, hours), F32),
            jax.ShapeDtypeStruct((rank, points), F32),
        ),
        in_specs=[vmem] * 8,
        out_specs=(vmem, vmem),
        scratch_shapes=[
            pltpu.VMEM((2, rank, 128), F32),
            pltpu.VMEM((lats, 2, rank, 128), F32),
            pltpu.VMEM((rank, 128), F32),
            pltpu.VMEM((2, rank, 128), F32),
            pltpu.VMEM((rank, 128), F32),
            pltpu.VMEM((tms, rank, 128), F32),
            pltpu.VMEM((rank, points), F32),
            pltpu.VMEM((rows, rank, WIDE), F32),
            pltpu.VMEM((tms, share, rank, WIDE), F32),
            pltpu.VMEM((extent, rank, WIDE), F32),
            pltpu.VMEM((extent, 2, 8, WIDE), F32),
            pltpu.VMEM((2, extent, rank, WIDE), F32),
            pltpu.VMEM((2, extent, rank, WIDE), F32),
            pltpu.VMEM((2, extent, rank, WIDE), F32),
            dma((lats,)), dma((lats,)), dma((2,)), dma((2,)), dma((2, 2)), dma((2, 2)),
            dma((tms,)), dma((tms,)), dma((tms,)), dma((tms,)), dma((tms,)), dma((tms,)),
            dma((2, tms)), dma((2, tms)),
        ],
        compiler_params=pltpu.CompilerParams(
            collective_id=0, has_side_effects=True, vmem_limit_bytes=56 * 2**20
        ),
    )(
        data.reshape(var_count * hours, points), space_init, time_init, variable_factor, neighbours,
        jnp.asarray(expand), jnp.asarray(tile), jnp.asarray(taps),
    )


def solution(mesh):
    placed = (P(None, "tm", "lat"), P(None, "lat"), P(None, "tm"), P(), P(None, "lat"))
    return jax.shard_map(
        functools.partial(per_device, mesh.shape["lat"], mesh.shape["tm"]),
        mesh=mesh,
        in_specs=placed,
        out_specs=(P(None, "tm"), P(None, "lat")),
        check_vma=False,
    )
```

time: 277 us -> 95.4 us (0.34)
  the two profiles are of different devices: /device:TPU:1 before, /device:TPU:25 now
where the time goes in v1:
time: 95.4 us; the launch traced here: 94.4 us
  Pallas kernels  89 us (93%)
  local copies, waits for them, and re-layouts  4.79 us (5%)
    pallas_call x1, Pallas kernels, per_device(): pl.pallas_call(functools.partial(kernel, lats, tms), out_shape=(jax.Shape...  89 us
    unnamed x2, local copies, waits for them, and re-layouts  3.4 us

profile of v1, /device:TPU:25, one launch (start us, length us, event | category | flops | bytes accessed | tf_op | source)
XLA Modules:
  0.0 94.4 jit_solution(13289747751325780484)
XLA Ops:
  0.6 1.4 %copy.10.time_ref = f32[32,16]{1,0:T(8,128)} copy(f32[32,16]{0,1:T(8,128)} %param.10) | data formatting | bytes 4096 | tf_op args[2]
  2.0 89.0 %shard_map.95 = (f32[32,16]{1,0:T(8,128)}, f32[32,5760]{1,0:T(8,128)}) custom-call(f32[128,5760]{1,0:T(8,128)} %bitcast.1, f32[32,5760]{1,0:T(8,128)} %space_ref.1, f32[32,16]{1,0:T(8,128)} %copy.10.time_ref, f32[8,32]{1,0:T(8,128)} %var_ref.1, s32[4,5760]{1,0:T(4,128)} %links_ref.1, f32[8,128]{1,0:T(8,128)} %constant.6.clone.expand_ref, ...), custom_call_target="tpu_custom_call" | custom-call | tf_op jit(solution)/shard_map/pallas_call | solution.py:354
  91.0 1.4 %copy.11 = f32[32,16]{0,1:T(8,128)} copy(f32[32,16]{1,0:T(8,128)} %get-tuple-element.2) | data formatting | bytes 4096 | tf_op jit(solution)/shard_map/pallas_call | solution.py:354
  92.4 2.0 %copy.13 = f32[32,5760]{1,0:T(8,128)} copy(f32[32,5760]{1,0:T(8,128)} %get-tuple-element.7) | data formatting | bytes 1474560

commit v2 on v1

--- a/solution.py
+++ b/solution.py
@@ -13,6 +13,7 @@
 WIDE = 384
 SIDE = (WIDE - NLON) // 2
 WINDOW = 512
+BATCH = 8
 F32 = jnp.float32
 BF16 = jnp.bfloat16
 HIGHEST = lax.Precision.HIGHEST
@@ -70,17 +71,19 @@
     lats, tms, data_ref, space_ref, time_ref, var_ref, links_ref, expand_ref, tile_ref, taps_ref,
     time_out, space_out,
     small, small_in, edge, edge_in, gram, gram_in, flat, terms, terms_in, rhs, codes,
-    centre, east, west,
+    centre, east, west, centre_b, east_b, west_b,
     small_s, small_r, edge_s, edge_r, halo_s, halo_r, gram_s, gram_r, rs_s, rs_r, ag_s, ag_r, fw_s, fw_r,
+    pair_in, partial, pair_s, pair_r, cross_s, cross_r,
 ):
     lat, tm = lax.axis_index("lat"), lax.axis_index("tm")
     rank, points = space_ref.shape
-    hours = time_ref.shape[1]
+    hours = time_ref.shape[0]
     rows = points // NLON
     deep = SWEEPS
     extent = rows + 2 * deep
     share = rows // tms
     north, south = lat > 0, lat < lats - 1
+    factors = ((centre, east, west), (centre_b, east_b, west_b))
 
     def to_lat(offset):
         return {"lat": lax.rem(lat + offset, lats)}
@@ -101,7 +104,7 @@
         pl.semaphore_signal(barrier, inc=1, device_id=to_tm(d), device_id_type=MESH)
 
     edge[...] = jnp.zeros_like(edge)
-    edge[:, :hours] = time_ref[...]
+    edge[:, :rank] = time_ref[...]
     pl.semaphore_wait(barrier, lats + tms - 2)
     up = send(edge, edge_in.at[0], edge_s.at[0], edge_r.at[0], to_tm(1))
     down = send(edge, edge_in.at[1], edge_s.at[1], edge_r.at[1], to_tm(tms - 1))
@@ -146,7 +149,7 @@
                 lambda s: flat[0:8, s : s + WINDOW], row, points, lane[:8]
             )
     for row in range(rows):
-        centre[0, deep + row] = spread_row(
+        centre[deep + row] = spread_row(
             lambda s: space_ref[:, s : s + WINDOW], row, points, lane
         )
     top, bottom = pl.ds(deep, deep), pl.ds(rows, deep)
@@ -155,7 +158,7 @@
     for side, (exists, mine, theirs, offset) in enumerate(
         ((north, top, behind_rows, lats - 1), (south, bottom, before, 1))
     ):
-        a = send(centre.at[0, mine], centre.at[0, theirs], halo_s.at[side, 0], halo_r.at[side, 0], to_lat(offset))
+        a = send(centre.at[mine], centre.at[theirs], halo_s.at[side, 0], halo_r.at[side, 0], to_lat(offset))
         b = send(codes.at[mine], codes.at[theirs], halo_s.at[side, 1], halo_r.at[side, 1], to_lat(offset))
         halo.append((exists, a, b))
 
@@ -170,10 +173,12 @@
     var_gram = exact_dot(var_ref[...], var_ref[...], TN)
     up.wait()
     down.wait()
-    past = jnp.where(tm > 0, edge_in[0, :, :hours], 0.0)
-    coming = jnp.where(tm < tms - 1, edge_in[1, :, :hours], 0.0)
+    past = jnp.where(tm > 0, edge_in[0, :, :rank], 0.0)
+    coming = jnp.where(tm < tms - 1, edge_in[1, :, :rank], 0.0)
     stencil = (
-        exact_dot(past, taps_ref[0]) + exact_dot(time_ref[...], taps_ref[1]) + exact_dot(coming, taps_ref[2])
+        exact_dot(past, taps_ref[0], TN)
+        + exact_dot(time_ref[...], taps_ref[1], TN)
+        + exact_dot(coming, taps_ref[2], TN)
     )
     total = small[...]
     for d, copy in enumerate(small_sends, 1):
@@ -182,7 +187,7 @@
     space_gram, time_rhs = total[0, :, :rank], total[1, :, :hours]
     time_inv = inverse(space_gram * var_gram + 3.0 * eye, row_id, col_id)
     time_factor = exact_dot(time_inv, time_rhs - 0.5 * stencil)
-    time_out[...] = time_factor
+    time_out[...] = exact_dot(time_factor, eye, TN)
     gram[...] = jnp.zeros_like(gram)
     gram[:, :rank] = exact_dot(time_factor, time_factor, NT)
     gram_sends = []
@@ -200,10 +205,24 @@
 
     for row in range(rows):
         terms[row] = spread_row(lambda s: flat[:, s : s + WINDOW], row, points, lane)
+    pairs = tms // 2
+    low = lax.rem(tm, 2)
+    other = {"tm": tm + 1 - 2 * low}
+
+    def block_of(k, side):
+        return lax.rem(tm // 2 + k, pairs) * 2 + side
+
+    order = [*range(1, pairs), 0]
+    pair_sends = {}
+    for k in order:
+        block = pl.ds(block_of(k, 1 - low) * share, share)
+        pair_sends[k] = send(terms.at[block], pair_in.at[k], pair_s.at[k], pair_r.at[k], other)
+        pair_sends[k].start()
     rs_sends = []
-    for d in range(1, tms):
-        target = lax.rem(tm + d, tms)
-        copy = send(terms.at[pl.ds(target * share, share)], terms_in.at[d], rs_s.at[d], rs_r.at[d], to_tm(d))
+    for k in range(1, pairs):
+        pair_sends[k].wait_recv()
+        partial[k] = terms[pl.ds(block_of(k, low) * share, share)] + pair_in[k]
+        copy = send(partial.at[k], terms_in.at[k], rs_s.at[k], rs_r.at[k], to_tm(2 * k))
         copy.start()
         rs_sends.append(copy)
 
@@ -218,22 +237,26 @@
     sweep_stack = left_stack(point_inv)
 
     mine = pl.ds(tm * share, share)
-    owned = terms[mine]
+    pair_sends[0].wait_recv()
+    owned = terms[mine] + pair_in[0]
     for d, copy in enumerate(rs_sends, 1):
         copy.wait_recv()
         owned = owned + terms_in[d]
     held = pl.ds(deep + tm * share, share)
     rhs[held] = owned / scale[None]
     ag_sends = []
-    for d in range(1, tms):
-        copy = send(rhs.at[held], rhs.at[held], ag_s.at[d], ag_r.at[d], to_tm(d))
+    for k in range(1, pairs):
+        copy = send(rhs.at[held], rhs.at[held], ag_s.at[k], ag_r.at[k], to_tm(2 * k))
         copy.start()
         ag_sends.append(copy)
 
-    def shift_row(buf, row):
-        cells = centre[buf, row]
-        east[buf, row] = pltpu.roll(cells, WIDE - 1, 1)
-        west[buf, row] = pltpu.roll(cells, 1, 1)
+    def across(k):
+        block = pl.ds(deep + block_of(pairs - k, low) * share, share)
+        copy = send(rhs.at[block], rhs.at[block], cross_s.at[k], cross_r.at[k], other)
+        copy.start()
+        return copy
+
+    cross_sends = [across(0)]
 
     for side, arrives in ((0, south), (1, north)):
         _, a, b = halo[side]
@@ -252,7 +275,9 @@
 
     @pl.loop(0, extent)
     def _(row):
-        shift_row(0, row)
+        cells = centre[row]
+        east[row] = pltpu.roll(cells, WIDE - 1, 1)
+        west[row] = pltpu.roll(cells, 1, 1)
 
     def forward(source, start):
         block = source * share
@@ -274,9 +299,13 @@
                     copy.wait_send()
 
     forward(tm, True)
-    for d, copy in enumerate(ag_sends, 1):
+    for k, copy in enumerate(ag_sends, 1):
         copy.wait_recv()
-        forward(lax.rem(tm + tms - d, tms), True)
+        cross_sends.append(across(k))
+        forward(block_of(pairs - k, low), True)
+    for k, copy in enumerate(cross_sends):
+        copy.wait_recv()
+        forward(block_of(pairs - k, 1 - low), True)
 
     for side, arrives in ((0, south), (1, north)):
         for source in range(tms):
@@ -292,44 +321,46 @@
                 def _(copy=copy):
                     copy.wait_recv()
 
-    def pick(buf, row, code):
-        a = centre[buf, row].reshape(rank // 8, 8, WIDE)
-        e = east[buf, row].reshape(rank // 8, 8, WIDE)
-        w = west[buf, row].reshape(rank // 8, 8, WIDE)
+    def pick(source, row, code):
+        a, e, w = (part[row].reshape(rank // 8, 8, WIDE) for part in source)
         code = code[None]
         moved = jnp.where(code == 1.0, e, jnp.where(code == 2.0, w, a))
         return jnp.where(code == 3.0, 0.0, moved)
 
     for sweep in range(SWEEPS):
-        now, later = sweep % 2, (sweep + 1) % 2
-        least = sweep + 1
-
-        def one(row, now=now, later=later, sweep=sweep):
-            sides = (east[now, row] + west[now, row]).reshape(rank // 8, 8, WIDE)
-            near = sides + pick(now, row - 1, codes[row, 0]) + pick(now, row + 1, codes[row, 1])
-            cells = split_dot(sweep_stack, rhs[row] + 0.5 * near.reshape(rank, WIDE))
-            centre[later, row] = cells
-            if sweep < SWEEPS - 1:
-                east[later, row] = pltpu.roll(cells, WIDE - 1, 1)
-                west[later, row] = pltpu.roll(cells, 1, 1)
-
-        @pl.loop(0, (extent - 2 * least) // 2)
-        def _(i, one=one, least=least):
-            one(least + 2 * i)
-            one(least + 2 * i + 1)
-
-    last = SWEEPS % 2
+        now, later = factors[sweep % 2], factors[(sweep + 1) % 2]
+        least, end = sweep + 1, extent - sweep - 1
+
+        def batch(first, now=now, later=later, sweep=sweep):
+            loads = []
+            for row in (first + i for i in range(BATCH)):
+                sides = (now[1][row] + now[2][row]).reshape(rank // 8, 8, WIDE)
+                near = sides + pick(now, row - 1, codes[row, 0]) + pick(now, row + 1, codes[row, 1])
+                loads.append(rhs[row] + 0.5 * near.reshape(rank, WIDE))
+            cells = split_dot(sweep_stack, jnp.concatenate(loads, axis=1))
+            for i in range(BATCH):
+                part = cells[:, i * WIDE : (i + 1) * WIDE]
+                later[0][first + i] = part
+                if sweep < SWEEPS - 1:
+                    later[1][first + i] = pltpu.roll(part, WIDE - 1, 1)
+                    later[2][first + i] = pltpu.roll(part, 1, 1)
+
+        @pl.loop(0, -(-(end - least) // BATCH))
+        def _(i, batch=batch, least=least, end=end):
+            batch(jnp.minimum(least + BATCH * i, end - BATCH))
+
+    last = factors[SWEEPS % 2][0]
     wide_lane = lax.broadcasted_iota(jnp.int32, (rank, WINDOW), 1)
     for row in range(rows):
         start, shift = window_of(row, points)
-        cells = jnp.concatenate([centre[last, deep + row], jnp.zeros((rank, WINDOW - WIDE), F32)], axis=1)
+        cells = jnp.concatenate([last[deep + row], jnp.zeros((rank, WINDOW - WIDE), F32)], axis=1)
         if shift:
             cells = pltpu.roll(cells, shift, 1)
         inside = (wide_lane >= shift) & (wide_lane < shift + NLON)
         old = space_out[:, start : start + WINDOW]
         space_out[:, start : start + WINDOW] = jnp.where(inside, cells, old)
 
-    for copy in rs_sends + ag_sends:
+    for copy in [*pair_sends.values(), *rs_sends, *ag_sends, *cross_sends]:
         copy.wait_send()
     for source in range(tms):
         forward(jnp.int32(source), False)
@@ -351,10 +382,10 @@
     taps = wide.reshape(3, hours, hours)
     vmem = pl.BlockSpec(memory_space=pltpu.VMEM)
     dma = pltpu.SemaphoreType.DMA
-    return pl.pallas_call(
+    time_factor, space_factor = pl.pallas_call(
         functools.partial(kernel, lats, tms),
         out_shape=(
-            jax.ShapeDtypeStruct((rank, hours), F32),
+            jax.ShapeDtypeStruct((hours, rank), F32),
             jax.ShapeDtypeStruct((rank, points), F32),
         ),
         in_specs=[vmem] * 8,
@@ -362,8 +393,8 @@
         scratch_shapes=[
             pltpu.VMEM((2, rank, 128), F32),
             pltpu.VMEM((lats, 2, rank, 128), F32),
-            pltpu.VMEM((rank, 128), F32),
-            pltpu.VMEM((2, rank, 128), F32),
+            pltpu.VMEM((hours, 128), F32),
+            pltpu.VMEM((2, hours, 128), F32),
             pltpu.VMEM((rank, 128), F32),
             pltpu.VMEM((tms, rank, 128), F32),
             pltpu.VMEM((rank, points), F32),
@@ -371,20 +402,27 @@
             pltpu.VMEM((tms, share, rank, WIDE), F32),
             pltpu.VMEM((extent, rank, WIDE), F32),
             pltpu.VMEM((extent, 2, 8, WIDE), F32),
-            pltpu.VMEM((2, extent, rank, WIDE), F32),
-            pltpu.VMEM((2, extent, rank, WIDE), F32),
-            pltpu.VMEM((2, extent, rank, WIDE), F32),
+            pltpu.VMEM((extent, rank, WIDE), F32),
+            pltpu.VMEM((extent, rank, WIDE), F32),
+            pltpu.VMEM((extent, rank, WIDE), F32),
+            pltpu.VMEM((extent, rank, WIDE), F32),
+            pltpu.VMEM((extent, rank, WIDE), F32),
+            pltpu.VMEM((extent, rank, WIDE), F32),
             dma((lats,)), dma((lats,)), dma((2,)), dma((2,)), dma((2, 2)), dma((2, 2)),
             dma((tms,)), dma((tms,)), dma((tms,)), dma((tms,)), dma((tms,)), dma((tms,)),
             dma((2, tms)), dma((2, tms)),
+            pltpu.VMEM((tms // 2, share, rank, WIDE), F32),
+            pltpu.VMEM((tms // 2, share, rank, WIDE), F32),
+            dma((tms // 2,)), dma((tms // 2,)), dma((tms // 2,)), dma((tms // 2,)),
         ],
         compiler_params=pltpu.CompilerParams(
             collective_id=0, has_side_effects=True, vmem_limit_bytes=56 * 2**20
         ),
     )(
-        data.reshape(var_count * hours, points), space_init, time_init, variable_factor, neighbours,
+        data.reshape(var_count * hours, points), space_init, time_init.T, variable_factor, neighbours,
         jnp.asarray(expand), jnp.asarray(tile), jnp.asarray(taps),
     )
+    return time_factor.T, space_factor
 
 
 def solution(mesh):

time: 95.4 us -> 71.8 us (0.75)
  Pallas kernels: 89 us -> 67.6 us
  local copies, waits for them, and re-layouts: 4.79 us -> 3.32 us
    pallas_call x1, Pallas kernels: 89 us -> 67.6 us  [per_device(): pl.pallas_call(functools.partial(kernel, lats, tms), out_shape=(jax.Shape...]
    pallas_call x1 -> x0, local copies, waits for them, and re-layouts: 1.39 us -> none  [per_device(): pl.pallas_call(functools.partial(kernel, lats, tms), out_shape=(jax.Shape...]
where the time goes in v2:
time: 71.8 us; the launch traced here: 71.5 us
  Pallas kernels  67.6 us (94%)
  local copies, waits for them, and re-layouts  3.32 us (5%)
    pallas_call x1, Pallas kernels, per_device(): pl.pallas_call(functools.partial(kernel, lats, tms), out_shape=(jax.Shape...  67.6 us
    unnamed x2, local copies, waits for them, and re-layouts  3.32 us

profile of v2, /device:TPU:25, one launch (start us, length us, event | category | flops | bytes accessed | tf_op | source)
XLA Modules:
  0.0 71.5 jit_solution(9726220545260398385)
XLA Ops:
  0.6 67.6 %shard_map.95 = (f32[16,32]{1,0:T(8,128)}, f32[32,5760]{1,0:T(8,128)}) custom-call(f32[128,5760]{1,0:T(8,128)} %bitcast.3, f32[32,5760]{1,0:T(8,128)} %space_ref.1, f32[16,32]{1,0:T(8,128)} %bitcast.4, f32[8,32]{1,0:T(8,128)} %var_ref.1, s32[4,5760]{1,0:T(4,128)} %links_ref.1, f32[8,128]{1,0:T(8,128)} %constant.6.clone.expand_ref, ...), custom_call_target="tpu_custom_call" | custom-call | tf_op jit(solution)/shard_map/pallas_call | solution.py:385
  68.2 1.3 %copy.12 = f32[32,16]{0,1:T(8,128)} copy(f32[32,16]{0,1:T(8,128)} %bitcast.5) | data formatting | bytes 4096
  69.5 2.0 %copy.13 = f32[32,5760]{1,0:T(8,128)} copy(f32[32,5760]{1,0:T(8,128)} %get-tuple-element.9) | data formatting | bytes 1474560

commit v3 on v2

--- a/solution.py
+++ b/solution.py
@@ -13,7 +13,7 @@
 WIDE = 384
 SIDE = (WIDE - NLON) // 2
 WINDOW = 512
-BATCH = 8
+BATCH = 10
 F32 = jnp.float32
 BF16 = jnp.bfloat16
 HIGHEST = lax.Precision.HIGHEST
@@ -330,24 +330,26 @@
     for sweep in range(SWEEPS):
         now, later = factors[sweep % 2], factors[(sweep + 1) % 2]
         least, end = sweep + 1, extent - sweep - 1
-
-        def batch(first, now=now, later=later, sweep=sweep):
+        steps = -(-(end - least) // BATCH)
+        size = -(-(end - least) // steps)
+
+        def batch(first, now=now, later=later, sweep=sweep, size=size):
             loads = []
-            for row in (first + i for i in range(BATCH)):
+            for row in (first + i for i in range(size)):
                 sides = (now[1][row] + now[2][row]).reshape(rank // 8, 8, WIDE)
                 near = sides + pick(now, row - 1, codes[row, 0]) + pick(now, row + 1, codes[row, 1])
                 loads.append(rhs[row] + 0.5 * near.reshape(rank, WIDE))
             cells = split_dot(sweep_stack, jnp.concatenate(loads, axis=1))
-            for i in range(BATCH):
+            for i in range(size):
                 part = cells[:, i * WIDE : (i + 1) * WIDE]
                 later[0][first + i] = part
                 if sweep < SWEEPS - 1:
                     later[1][first + i] = pltpu.roll(part, WIDE - 1, 1)
                     later[2][first + i] = pltpu.roll(part, 1, 1)
 
-        @pl.loop(0, -(-(end - least) // BATCH))
-        def _(i, batch=batch, least=least, end=end):
-            batch(jnp.minimum(least + BATCH * i, end - BATCH))
+        @pl.loop(0, steps)
+        def _(i, batch=batch, least=least, end=end, size=size):
+            batch(jnp.minimum(least + size * i, end - size))
 
     last = factors[SWEEPS % 2][0]
     wide_lane = lax.broadcasted_iota(jnp.int32, (rank, WINDOW), 1)

time: 71.8 us -> 70.1 us (0.976)
  Pallas kernels: 67.6 us -> 65.9 us
    pallas_call x1, Pallas kernels: 67.6 us -> 65.9 us  [per_device(): pl.pallas_call(functools.partial(kernel, lats, tms), out_shape=(jax.Shape...]
where the time goes in v3:
time: 70.1 us; the launch traced here: 69.9 us
  Pallas kernels  65.9 us (94%)
  local copies, waits for them, and re-layouts  3.32 us (5%)
    pallas_call x1, Pallas kernels, per_device(): pl.pallas_call(functools.partial(kernel, lats, tms), out_shape=(jax.Shape...  65.9 us
    unnamed x2, local copies, waits for them, and re-layouts  3.32 us

profile of v3, /device:TPU:25, one launch (start us, length us, event | category | flops | bytes accessed | tf_op | source)
XLA Modules:
  0.0 69.9 jit_solution(14931078782536894884)
XLA Ops:
  0.6 65.9 %shard_map.95 = (f32[16,32]{1,0:T(8,128)}, f32[32,5760]{1,0:T(8,128)}) custom-call(f32[128,5760]{1,0:T(8,128)} %bitcast.3, f32[32,5760]{1,0:T(8,128)} %space_ref.1, f32[16,32]{1,0:T(8,128)} %bitcast.4, f32[8,32]{1,0:T(8,128)} %var_ref.1, s32[4,5760]{1,0:T(4,128)} %links_ref.1, f32[8,128]{1,0:T(8,128)} %constant.6.clone.expand_ref, ...), custom_call_target="tpu_custom_call" | custom-call | tf_op jit(solution)/shard_map/pallas_call | solution.py:387
  66.6 1.3 %copy.12 = f32[32,16]{0,1:T(8,128)} copy(f32[32,16]{0,1:T(8,128)} %bitcast.5) | data formatting | bytes 4096
  67.9 2.0 %copy.13 = f32[32,5760]{1,0:T(8,128)} copy(f32[32,5760]{1,0:T(8,128)} %get-tuple-element.9) | data formatting | bytes 1474560
